TPU v7x, 128 devices: a whole 4x4x4 slice. The times are simulated.
128 devices in a mesh: row: 16 (over y, x), col: 8 (over z, core).
Axes of the slice: x: 4, y: 4, z: 4, core: 2. Of those that a mesh axis runs over, the one named last changes fastest.
Arguments:
- inputs: bfloat16 [1024, 8192], P('col', 'row'), may hold values from -6 to 6
- out_grad: bfloat16 [1024, 8192], P('col', 'row'), may hold values from -1.5 to 1.5
- gate_pre: bfloat16 [1024, 14336], P('row', 'col'), may hold values from -9 to 9
- up_pre: bfloat16 [1024, 14336], P('row', 'col'), may hold values from -6 to 6
- gate_weight: bfloat16 [8192, 14336], P('row', 'col'), may hold values from -0.0625 to 0.0625
- up_weight: bfloat16 [8192, 14336], P('row', 'col'), may hold values from -0.0625 to 0.0625
- down_weight: bfloat16 [14336, 8192], P('col', 'row'), may hold values from -0.046875 to 0.046875
Outputs:
- input_grad: float32 [1024, 8192], P('col', 'row')
- gate_grad: float32 [8192, 14336], P('row', 'col')
- up_grad: float32 [8192, 14336], P('row', 'col')
- down_grad: float32 [14336, 8192], P('col', 'row')
All inputs are finite; a program needn't handle non-finite values.
Results may differ from a plain program's by a relative error of at most 0.0029.
Values may be sent and summed in bfloat16 or wider, within the bound.
A program may use at most 128 MiB of HBM per device.

v0:
```python
import jax
import jax.numpy as jnp
from jax import lax
from jax.sharding import PartitionSpec as P

LEAD_DIMS = (((0,), (0,)), ((), ()))
LAST_DIMS = (((1,), (1,)), ((), ()))


def swiglu_grads(grad_hidden, gate_pre, up_pre):
    gate_val = gate_pre.astype(jnp.float32)
    up_val = up_pre.astype(jnp.float32)
    gate_sig = jax.nn.sigmoid(gate_val)
    hidden = (gate_val * gate_sig * up_val).astype(jnp.bfloat16)
    grad_gate = (grad_hidden * up_val * gate_sig * (1.0 + gate_val * (1.0 - gate_sig))).astype(
        jnp.bfloat16
    )
    grad_up = (grad_hidden * gate_val * gate_sig).astype(jnp.bfloat16)
    return (hidden, grad_gate, grad_up)


def body(inputs, out_grad, gate_pre, up_pre, gate_weight, up_weight, down_weight):
    input_full, grad_full = (
        lax.all_gather(inputs, "col", axis=0, tiled=True),
        lax.all_gather(out_grad, "col", axis=0, tiled=True),
    )
    partial_sum = lax.dot_general(
        grad_full, down_weight, LAST_DIMS, preferred_element_type=jnp.float32
    )
    grad_hidden = lax.psum(partial_sum, "row")
    gate_all, up_all = (
        lax.all_gather(gate_pre, "row", axis=0, tiled=True),
        lax.all_gather(up_pre, "row", axis=0, tiled=True),
    )
    hidden, grad_gate, grad_up = swiglu_grads(grad_hidden, gate_all, up_all)
    total = lax.dot_general(grad_gate, gate_weight, LAST_DIMS, preferred_element_type=jnp.float32)
    input_grad = lax.psum_scatter(
        total + lax.dot_general(grad_up, up_weight, LAST_DIMS, preferred_element_type=jnp.float32),
        "col",
        scatter_dimension=0,
        tiled=True,
    )
    gate_grad = lax.dot_general(
        input_full, grad_gate, LEAD_DIMS, preferred_element_type=jnp.float32
    )
    up_grad = lax.dot_general(input_full, grad_up, LEAD_DIMS, preferred_element_type=jnp.float32)
    down_grad = lax.dot_general(hidden, grad_full, LEAD_DIMS, preferred_element_type=jnp.float32)
    return (input_grad, gate_grad, up_grad, down_grad)


def solution(mesh):
    in_specs = (
        P("col", "row"),
        P("col", "row"),
        P("row", "col"),
        P("row", "col"),
        P("row", "col"),
        P("row", "col"),
        P("col", "row"),
    )
    out_specs = (P("col", "row"), P("row", "col"), P("row", "col"), P("col", "row"))
    return jax.shard_map(body, mesh=mesh, in_specs=in_specs, out_specs=out_specs, check_vma=False)
```

profile of v0, /device:TPU:0, one launch (start us, length us, event | category | flops | bytes accessed | tf_op | source)
XLA Modules:
  0.0 340.9 jit_solution(9743817639233089111)
XLA Ops:
  7.2 0.0 copy-start
  7.2 0.0 all-gather.5.cloned.1.call-start
  7.2 0.7 all-gather.5.cloned.1.call-update
  7.9 0.0 all-gather.7.cloned.1.call-start
  8.0 0.7 all-gather.7.cloned.1.call-update
  8.7 0.0 all-gather.9.cloned.1.call-start
  8.7 0.7 all-gather.9.cloned.1.call-update
  9.4 0.0 all-reduce.2.cloned.1.call-start
  9.4 26.4 %all-gather.5.cloned.1.call-done = bf16[1024,512]{1,0:T(8,128)(2,1)} async-done(((bf16[128,512]{1,0:T(8,128)(2,1)}), bf16[1024,512]{1,0:T(8,128)(2,1)}) %all-gather.5.cloned.1.call-update) | async-done | bytes 1048592 | tf_op jit(solution)/shard_map/all_gather | solution.py:25
  35.8 0.0 copy-done
  35.8 6.4 %fusion.13 = f32[1024,1792]{1,0:T(8,128)} fusion(bf16[1024,512]{1,0:T(8,128)(2,1)} %all-gather.5.cloned.1.call-done, bf16[1792,512]{1,0:T(8,128)(2,1)S(1)} %copy-done), kind=kOutput, calls=%fused_computation.21 | convolution fusion | flops 1879048192 | bytes 10223616 | tf_op jit(solution)/shard_map/dot_general | solution.py:27
  42.2 0.0 all-reduce.2.cloned.1.call-update
  42.2 0.0 all-gather.11.cloned.1.call-start
  42.2 0.5 all-gather.11.cloned.1.call-update
  42.8 0.0 reduce-scatter.2.cloned.1.call-start
  42.8 44.6 %all-gather.7.cloned.1.call-done = bf16[1024,1792]{1,0:T(8,128)(2,1)} async-done(((bf16[64,1792]{1,0:T(8,128)(2,1)}), bf16[1024,1792]{1,0:T(8,128)(2,1)}) %all-gather.7.cloned.1.call-update) | async-done | bytes 3670032 | tf_op jit(solution)/shard_map/all_gather | solution.py:33
  87.4 50.9 %all-gather.9.cloned.1.call-done = bf16[1024,1792]{1,0:T(8,128)(2,1)} async-done(((bf16[64,1792]{1,0:T(8,128)(2,1)}), bf16[1024,1792]{1,0:T(8,128)(2,1)}) %all-gather.9.cloned.1.call-update) | async-done | bytes 3670032 | tf_op jit(solution)/shard_map/all_gather | solution.py:32
  138.3 133.8 %all-reduce.2.cloned.1.call-done = f32[1024,1792]{1,0:T(8,128)} async-done(((f32[1024,1792]{1,0:T(8,128)}), f32[1024,1792]{1,0:T(8,128)}) %all-reduce.2.cloned.1.call-update) | async-done | bytes 7340048 | tf_op jit(solution)/shard_map/psum | solution.py:30
  272.2 0.0 copy-start.3
  272.2 7.1 %fusion.9 = (bf16[1024,1792]{1,0:T(8,128)(2,1)S(1)}, bf16[1024,1792]{1,0:T(8,128)(2,1)S(1)}) fusion(f32[1024,1792]{1,0:T(8,128)} %all-reduce.2.cloned.1.call-done, bf16[1024,1792]{1,0:T(8,128)(2,1)} %all-gather.9.cloned.1.call-done, bf16[1024,1792]{1,0:T(8,128)(2,1)} %all-gather.7.cloned.1.call-done), kind=kLoop, calls=%fused_computation.15 | loop fusion | flops 27525120 | bytes 22020096 | tf_op jit(solution)/shard_map/convert_element_type | solution.py:18
  279.3 0.0 copy-start.2
  279.3 0.0 copy-start.1
  279.3 0.0 copy-done.3
  279.3 0.0 copy-start.4
  279.4 2.1 fusion.14
  281.4 0.0 copy-done.2
  281.5 1.1 copy-done.1
  282.5 0.0 copy-done.4
  282.5 0.0 copy-start.5
  282.5 3.5 %convolution_add_fusion = f32[1024,512]{1,0:T(8,128)} fusion(f32[1024,512]{1,0:T(8,128)S(1)} %fusion.14, bf16[1024,1792]{1,0:T(8,128)(2,1)S(1)} %get-tuple-element.8, bf16[512,1792]{1,0:T(8,128)(2,1)S(1)} %copy-done.4), kind=kOutput, calls=%fused_computation.19 | convolution fusion | flops 1879572480 | bytes 9699328 | tf_op jit(solution)/shard_map/dot_general | solution.py:38
  286.0 0.0 reduce-scatter.2.cloned.1.call-update
  286.0 0.0 copy-done.5
  286.0 7.8 %fusion.10 = f32[1792,512]{1,0:T(8,128)} fusion(bf16[1024,512]{1,0:T(8,128)(2,1)S(1)} %copy-done.5, bf16[1024,1792]{1,0:T(8,128)(2,1)} %all-gather.7.cloned.1.call-done, bf16[1024,1792]{1,0:T(8,128)(2,1)} %all-gather.9.cloned.1.call-done), kind=kOutput, calls=%fused_computation.16 | convolution fusion | flops 1893728256 | bytes 12058624 | tf_op jit(solution)/shard_map/dot_general | solution.py:47
  293.9 3.4 all-gather.11.cloned.1.call-done
  297.3 6.3 %convolution_bitcast_fusion.1 = f32[512,1792]{0,1:T(8,128)} fusion(bf16[1024,1792]{1,0:T(8,128)(2,1)} %copy-done.2, bf16[1024,512]{1,0:T(8,128)(2,1)} %all-gather.11.cloned.1.call-done), kind=kOutput, calls=%fused_computation.18 | convolution fusion | flops 1879048192 | bytes 8388608 | tf_op jit(solution)/shard_map/dot_general | solution.py:43
  303.5 0.0 copy-start.6
  303.5 5.2 %copy.11 = f32[512,1792]{1,0:T(8,128)} copy(f32[512,1792]{0,1:T(8,128)} %convolution_bitcast_fusion.1) | data formatting | bytes 7340032
  308.7 0.0 copy-done.6
  308.7 6.0 %convolution_bitcast_fusion = f32[512,1792]{0,1:T(8,128)} fusion(bf16[1024,1792]{1,0:T(8,128)(2,1)} %copy-done.1, bf16[1024,512]{1,0:T(8,128)(2,1)S(1)} %copy-done.6), kind=kOutput, calls=%fused_computation.17 | convolution fusion | flops 1879048192 | bytes 8388608 | tf_op jit(solution)/shard_map/dot_general | solution.py:46
  314.7 5.2 %copy.12 = f32[512,1792]{1,0:T(8,128)} copy(f32[512,1792]{0,1:T(8,128)} %convolution_bitcast_fusion) | data formatting | bytes 7340032
  319.9 14.1 %reduce-scatter.2.cloned.1.call-done = f32[128,512]{1,0:T(8,128)} async-done(((f32[1024,512]{1,0:T(8,128)}), f32[128,512]{1,0:T(8,128)}) %reduce-scatter.2.cloned.1.call-update) | async-done | bytes 262160 | tf_op jit(solution)/shard_map/reduce_scatter | solution.py:37
Async XLA Ops:
  7.2 28.6 %copy-start = (bf16[1792,512]{1,0:T(8,128)(2,1)S(1)}, bf16[1792,512]{1,0:T(8,128)(2,1)}, u32[]{:S(2)}) copy-start(bf16[1792,512]{1,0:T(8,128)(2,1)} %param.13) | copy-start | bytes 5505028
  7.2 28.6 %all-gather.5.cloned.1.call-start = ((), (), s32[]{:S(2)}) async-start(), calls=%async_computation.1 | async-start | bytes 1179648 | tf_op jit(solution)/shard_map/all_gather | solution.py:25
  7.9 79.5 %all-gather.7.cloned.1.call-start = ((), (), s32[]{:S(2)}) async-start(), calls=%async_computation.3 | async-start | bytes 3899392 | tf_op jit(solution)/shard_map/all_gather | solution.py:33
  8.7 129.7 %all-gather.9.cloned.1.call-start = ((), (), s32[]{:S(2)}) async-start(), calls=%async_computation.4 | async-start | bytes 3899392 | tf_op jit(solution)/shard_map/all_gather | solution.py:32
  9.4 262.8 %all-reduce.2.cloned.1.call-start = ((), (), s32[]{:S(2)}) async-start(), calls=%async_computation.2 | async-start | bytes 14680064 | tf_op jit(solution)/shard_map/psum | solution.py:30
  42.2 255.1 %all-gather.11.cloned.1.call-start = ((), (), s32[]{:S(2)}) async-start(), calls=%async_computation.6 | async-start | bytes 1179648 | tf_op jit(solution)/shard_map/all_gather | solution.py:24
  42.8 291.3 %reduce-scatter.2.cloned.1.call-start = ((), (), s32[]{:S(2)}) async-start(), calls=%async_computation.5 | async-start | bytes 2359296 | tf_op jit(solution)/shard_map/reduce_scatter | solution.py:37
  272.2 7.2 %copy-start.3 = (bf16[512,1792]{1,0:T(8,128)(2,1)S(1)}, bf16[512,1792]{1,0:T(8,128)(2,1)}, u32[]{:S(2)}) copy-start(bf16[512,1792]{1,0:T(8,128)(2,1)} %param.11) | copy-start | bytes 5505028
  279.3 2.1 copy-start.2
  279.3 3.2 copy-start.1
  279.3 3.2 copy-start.4
  282.5 3.5 %copy-start.5 = (bf16[1024,512]{1,0:T(8,128)(2,1)S(1)}, bf16[1024,512]{1,0:T(8,128)(2,1)}, u32[]{:S(2)}) copy-start(bf16[1024,512]{1,0:T(8,128)(2,1)} %all-gather.5.cloned.1.call-done) | copy-start | bytes 3145732
  303.5 5.2 %copy-start.6 = (bf16[1024,512]{1,0:T(8,128)(2,1)S(1)}, bf16[1024,512]{1,0:T(8,128)(2,1)}, u32[]{:S(2)}) copy-start(bf16[1024,512]{1,0:T(8,128)(2,1)} %all-gather.11.cloned.1.call-done) | copy-start | bytes 3145732
Sparse Core Ops, SparseCore 0:
  9.7 26.0 all-gather.4
  37.9 49.4 all-gather.6
  89.5 48.7 all-gather.8
  141.6 130.4 all-reduce.1
  273.8 23.3 all-gather.10
  300.2 33.7 reduce-scatter.1
where the time goes:
time: 341 us
  waiting for transfers between devices  276 us (81%)
  matrix products  32 us (9%)
  between operations  14.2 us (4%)
  local copies, waits for them, and re-layouts  11.4 us (3%)
  other arithmetic  7.15 us (2%)
    psum x1, waiting for transfers between devices, body(): grad_hidden = lax.psum(partial_sum, 'row')  134 us
    all_gather x1, waiting for transfers between devices, body(): lax.all_gather(gate_pre, 'row', axis=0, tiled=True)  50.9 us
    all_gather x1, waiting for transfers between devices, body(): lax.all_gather(up_pre, 'row', axis=0, tiled=True)  44.6 us
    all_gather x1, waiting for transfers between devices, body(): lax.all_gather(out_grad, 'col', axis=0, tiled=True)  26.4 us
    reduce_scatter x1, waiting for transfers between devices, body(): lax.psum_scatter(total + lax.dot_general(grad_up, up_weight, LAST_DIMS, p...  14.1 us
    unnamed x16, local copies, waits for them, and re-layouts  11.4 us
    dot_general x1, matrix products, body(): lax.dot_general(hidden, grad_full, LEAD_DIMS, preferred_element_type=jnp....  7.83 us
    convert_element_type x1, other arithmetic, swiglu_grads(): grad_up = (grad_hidden * gate_val * gate_sig).astype(jnp.bfloat16)  7.15 us
  transfers between devices with their start and end apart: 6, of which 6 were waited for; matrix products, arithmetic and copies ran while one was open for 15% of the time, Pallas kernels for 0%

commit v1 on v0

v1 whole, which is shorter than its diff:
```python
import jax
import jax.numpy as jnp
from jax import lax
from jax.sharding import PartitionSpec as P

LEAD_DIMS = (((0,), (0,)), ((), ()))
LAST_DIMS = (((1,), (1,)), ((), ()))


def body(inputs, out_grad, gate_pre, up_pre, gate_weight, up_weight, down_weight):
    gate_val = gate_pre.astype(jnp.float32)
    up_val = up_pre.astype(jnp.float32)
    gate_sig = jax.nn.sigmoid(gate_val)
    hidden = (gate_val * gate_sig * up_val).astype(jnp.bfloat16)
    grad_full = lax.all_gather(out_grad, "col", axis=0, tiled=True)
    hidden_all = lax.all_gather(hidden, "row", axis=0, tiled=True)
    partial_sum = lax.dot_general(
        grad_full, down_weight, LAST_DIMS, preferred_element_type=jnp.float32
    )
    grad_hidden = lax.psum_scatter(partial_sum, "row", scatter_dimension=0, tiled=True)
    input_full = lax.all_gather(inputs, "col", axis=0, tiled=True)
    grad_gate = (
        grad_hidden * up_val * gate_sig * (1.0 + gate_val * (1.0 - gate_sig))
    ).astype(jnp.bfloat16)
    grad_up = (grad_hidden * gate_val * gate_sig).astype(jnp.bfloat16)
    down_grad = lax.dot_general(
        hidden_all, grad_full, LEAD_DIMS, preferred_element_type=jnp.float32
    )
    gate_all = lax.all_gather(grad_gate, "row", axis=0, tiled=True)
    up_all = lax.all_gather(grad_up, "row", axis=0, tiled=True)
    total = lax.dot_general(gate_all, gate_weight, LAST_DIMS, preferred_element_type=jnp.float32)
    input_grad = lax.psum_scatter(
        total + lax.dot_general(up_all, up_weight, LAST_DIMS, preferred_element_type=jnp.float32),
        "col",
        scatter_dimension=0,
        tiled=True,
    )
    gate_grad = lax.dot_general(input_full, gate_all, LEAD_DIMS, preferred_element_type=jnp.float32)
    up_grad = lax.dot_general(input_full, up_all, LEAD_DIMS, preferred_element_type=jnp.float32)
    return (input_grad, gate_grad, up_grad, down_grad)


def solution(mesh):
    in_specs = (
        P("col", "row"),
        P("col", "row"),
        P("row", "col"),
        P("row", "col"),
        P("row", "col"),
        P("row", "col"),
        P("col", "row"),
    )
    out_specs = (P("col", "row"), P("row", "col"), P("row", "col"), P("col", "row"))
    return jax.shard_map(body, mesh=mesh, in_specs=in_specs, out_specs=out_specs, check_vma=False)
```

time: 341 us -> 348 us (1.021)
  waiting for transfers between devices: 276 us -> 283 us
  matrix products: 32 us -> 37.4 us
  other arithmetic: 7.15 us -> 2.09 us
    psum x1 -> x0, waiting for transfers between devices: 134 us -> none  [body(): grad_hidden = lax.psum(partial_sum, 'row')]
    reduce_scatter x1 -> x2, waiting for transfers between devices: 14.1 us -> 113 us  [the longest x1 82.8 us: body(): lax.psum_scatter(partial_sum, 'row', scatter_dimension=0, tiled=True)]
    all_gather x4 -> x5, waiting for transfers between devices: 125 us -> 168 us  [the longest x1 47.9 us: body(): gate_all = lax.all_gather(grad_gate, 'row', axis=0, tiled=True)]
    dot_general x5, matrix products: 25.7 us -> 31.1 us  [the longest x1 6.74 us: body(): lax.dot_general(up_all, up_weight, LAST_DIMS, preferred_element_type=jnp....]
    convert_element_type x1, other arithmetic: 7.15 us -> 2.09 us  [body(): grad_up = (grad_hidden * gate_val * gate_sig).astype(jnp.bfloat16)]
    unnamed x16 -> x12, local copies, waits for them, and re-layouts: 11.4 us -> 10.5 us
  transfers between devices with their start and end apart: 6 -> 7, of which waited for: 6 -> 7; matrix products, arithmetic and copies ran while one was open for 15% -> 12% of each run, Pallas kernels for 0% -> 0%
where the time goes in v1:
time: 348 us; the launch traced here: 347 us
  waiting for transfers between devices  283 us (81%)
  matrix products  37.4 us (11%)
  between operations  14.1 us (4%)
  local copies, waits for them, and re-layouts  10.5 us (3%)
    reduce_scatter x1, waiting for transfers between devices, body(): lax.psum_scatter(partial_sum, 'row', scatter_dimension=0, tiled=True)  82.8 us
    all_gather x1, waiting for transfers between devices, body(): gate_all = lax.all_gather(grad_gate, 'row', axis=0, tiled=True)  47.9 us
    all_gather x1, waiting for transfers between devices, body(): up_all = lax.all_gather(grad_up, 'row', axis=0, tiled=True)  45.6 us
    reduce_scatter x1, waiting for transfers between devices, body(): lax.psum_scatter(total + lax.dot_general(up_all, up_weight, LAST_DIMS, pr...  30.2 us
    all_gather x1, waiting for transfers between devices, body(): hidden_all = lax.all_gather(hidden, 'row', axis=0, tiled=True)  28.9 us
    all_gather x1, waiting for transfers between devices, body(): grad_full = lax.all_gather(out_grad, 'col', axis=0, tiled=True)  27.8 us
    all_gather x1, waiting for transfers between devices, body(): input_full = lax.all_gather(inputs, 'col', axis=0, tiled=True)  17.7 us
    unnamed x12, local copies, waits for them, and re-layouts  10.5 us
  transfers between devices with their start and end apart: 7, of which 7 were waited for; matrix products, arithmetic and copies ran while one was open for 12% of the time, Pallas kernels for 0%

profile of v1, /device:TPU:0, one launch (start us, length us, event | category | flops | bytes accessed | tf_op | source)
XLA Modules:
  0.0 347.5 jit_solution(18138531377756682958)
XLA Ops:
  7.2 0.0 copy-start
  7.2 0.0 all-gather.6.cloned.1.call-start
  7.2 0.7 all-gather.6.cloned.1.call-update
  7.9 0.0 reduce-scatter.3.cloned.1.call-start
  8.0 27.8 %all-gather.6.cloned.1.call-done = bf16[1024,512]{1,0:T(8,128)(2,1)} async-done(((bf16[128,512]{1,0:T(8,128)(2,1)}), bf16[1024,512]{1,0:T(8,128)(2,1)}) %all-gather.6.cloned.1.call-update) | async-done | bytes 1048592 | tf_op jit(solution)/shard_map/all_gather | solution.py:15
  35.8 0.0 copy-done
  35.8 6.3 %fusion.10 = f32[1024,1792]{1,0:T(8,128)} fusion(bf16[1024,512]{1,0:T(8,128)(2,1)} %all-gather.6.cloned.1.call-done, bf16[1792,512]{1,0:T(8,128)(2,1)S(1)} %copy-done), kind=kOutput, calls=%fused_computation.19 | convolution fusion | flops 1879048192 | bytes 10223616 | tf_op jit(solution)/shard_map/dot_general | solution.py:17
  42.1 0.0 copy-start.1
  42.1 0.0 copy-start.2
  42.1 0.0 reduce-scatter.3.cloned.1.call-update
  42.1 0.0 all-gather.8.cloned.1.call-start
  42.2 82.8 %reduce-scatter.3.cloned.1.call-done = f32[64,1792]{1,0:T(8,128)} async-done(((f32[1024,1792]{1,0:T(8,128)}), f32[64,1792]{1,0:T(8,128)}) %reduce-scatter.3.cloned.1.call-update) | async-done | bytes 458768 | tf_op jit(solution)/shard_map/reduce_scatter | solution.py:20
  124.9 0.0 copy-done.1
  124.9 0.0 copy-done.2
  124.9 2.1 fusion.9
  127.0 0.0 all-gather.8.cloned.1.call-update
  127.0 0.0 all-gather.10.cloned.1.call-start
  127.1 0.5 all-gather.10.cloned.1.call-update
  127.6 0.0 all-gather.12.cloned.1.call-start
  127.7 0.5 all-gather.12.cloned.1.call-update
  128.2 0.0 all-gather.14.cloned.1.call-start
  128.2 0.5 all-gather.14.cloned.1.call-update
  128.8 0.0 reduce-scatter.5.cloned.1.call-start
  128.8 47.9 %all-gather.8.cloned.1.call-done = bf16[1024,1792]{1,0:T(8,128)(2,1)} async-done(((bf16[64,1792]{1,0:T(8,128)(2,1)}), bf16[1024,1792]{1,0:T(8,128)(2,1)}) %all-gather.8.cloned.1.call-update) | async-done | bytes 3670032 | tf_op jit(solution)/shard_map/all_gather | solution.py:29
  176.7 6.0 %fusion.11 = f32[1024,512]{1,0:T(8,128)} fusion(bf16[1024,1792]{1,0:T(8,128)(2,1)} %all-gather.8.cloned.1.call-done, bf16[512,1792]{1,0:T(8,128)(2,1)} %param.11), kind=kOutput, calls=%fused_computation.20 | convolution fusion | flops 1879048192 | bytes 7602176 | tf_op jit(solution)/shard_map/dot_general | solution.py:31
  182.8 45.6 %all-gather.10.cloned.1.call-done = bf16[1024,1792]{1,0:T(8,128)(2,1)} async-done(((bf16[64,1792]{1,0:T(8,128)(2,1)}), bf16[1024,1792]{1,0:T(8,128)(2,1)}) %all-gather.10.cloned.1.call-update) | async-done | bytes 3670032 | tf_op jit(solution)/shard_map/all_gather | solution.py:30
  228.3 6.7 %convolution_add_fusion = f32[1024,512]{1,0:T(8,128)} fusion(f32[1024,512]{1,0:T(8,128)} %fusion.11, bf16[1024,1792]{1,0:T(8,128)(2,1)} %all-gather.10.cloned.1.call-done, bf16[512,1792]{1,0:T(8,128)(2,1)} %param.12), kind=kOutput, calls=%fused_computation.2 | convolution fusion | flops 1879572480 | bytes 9699328 | tf_op jit(solution)/shard_map/dot_general | solution.py:33
  235.1 0.0 reduce-scatter.5.cloned.1.call-update
  235.1 17.7 %all-gather.12.cloned.1.call-done = bf16[1024,512]{1,0:T(8,128)(2,1)} async-done(((bf16[128,512]{1,0:T(8,128)(2,1)}), bf16[1024,512]{1,0:T(8,128)(2,1)}) %all-gather.12.cloned.1.call-update) | async-done | bytes 1048592 | tf_op jit(solution)/shard_map/all_gather | solution.py:21
  252.8 6.3 %convolution_bitcast_fusion.1 = f32[512,1792]{0,1:T(8,128)} fusion(bf16[1024,1792]{1,0:T(8,128)(2,1)} %all-gather.8.cloned.1.call-done, bf16[1024,512]{1,0:T(8,128)(2,1)} %all-gather.12.cloned.1.call-done), kind=kOutput, calls=%fused_computation.1 | convolution fusion | flops 1879048192 | bytes 8388608 | tf_op jit(solution)/shard_map/dot_general | solution.py:38
  259.1 0.0 copy-start.4
  259.1 5.2 %copy.11 = f32[512,1792]{1,0:T(8,128)} copy(f32[512,1792]{0,1:T(8,128)} %convolution_bitcast_fusion.1) | data formatting | bytes 7340032
  264.3 0.0 copy-done.4
  264.3 6.1 %convolution_bitcast_fusion = f32[512,1792]{0,1:T(8,128)} fusion(bf16[1024,1792]{1,0:T(8,128)(2,1)} %all-gather.10.cloned.1.call-done, bf16[1024,512]{1,0:T(8,128)(2,1)S(1)} %copy-done.4), kind=kOutput, calls=%fused_computation | convolution fusion | flops 1879048192 | bytes 8388608 | tf_op jit(solution)/shard_map/dot_general | solution.py:39
  270.4 0.0 copy-start.3
  270.4 5.2 %copy.12 = f32[512,1792]{1,0:T(8,128)} copy(f32[512,1792]{0,1:T(8,128)} %convolution_bitcast_fusion) | data formatting | bytes 7340032
  275.7 28.9 %all-gather.14.cloned.1.call-done = bf16[1024,1792]{1,0:T(8,128)(2,1)} async-done(((bf16[64,1792]{1,0:T(8,128)(2,1)}), bf16[1024,1792]{1,0:T(8,128)(2,1)}) %all-gather.14.cloned.1.call-update) | async-done | bytes 3670032 | tf_op jit(solution)/shard_map/all_gather | solution.py:16
  304.5 0.0 copy-done.3
  304.5 6.0 %fusion.12 = f32[1792,512]{1,0:T(8,128)} fusion(bf16[1024,1792]{1,0:T(8,128)(2,1)} %all-gather.14.cloned.1.call-done, bf16[1024,512]{1,0:T(8,128)(2,1)S(1)} %copy-done.3), kind=kOutput, calls=%fused_computation.21 | convolution fusion | flops 1879048192 | bytes 8388608 | tf_op jit(solution)/shard_map/dot_general | solution.py:26
  310.5 30.2 %reduce-scatter.5.cloned.1.call-done = f32[128,512]{1,0:T(8,128)} async-done(((f32[1024,512]{1,0:T(8,128)}), f32[128,512]{1,0:T(8,128)}) %reduce-scatter.5.cloned.1.call-update) | async-done | bytes 262160 | tf_op jit(solution)/shard_map/reduce_scatter | solution.py:32
Async XLA Ops:
  7.2 28.6 %copy-start = (bf16[1792,512]{1,0:T(8,128)(2,1)S(1)}, bf16[1792,512]{1,0:T(8,128)(2,1)}, u32[]{:S(2)}) copy-start(bf16[1792,512]{1,0:T(8,128)(2,1)} %param.13) | copy-start | bytes 5505028
  7.2 28.6 %all-gather.6.cloned.1.call-start = ((), (), s32[]{:S(2)}) async-start(), calls=%async_computation.2 | async-start | bytes 1179648 | tf_op jit(solution)/shard_map/all_gather | solution.py:15
  7.9 117.0 %reduce-scatter.3.cloned.1.call-start = ((), (), s32[]{:S(2)}) async-start(), calls=%async_computation.3 | async-start | bytes 7798784 | tf_op jit(solution)/shard_map/reduce_scatter | solution.py:20
  42.1 82.8 %copy-start.1 = (bf16[64,1792]{1,0:T(8,128)(2,1)S(1)}, bf16[64,1792]{1,0:T(8,128)(2,1)}, u32[]{:S(2)}) copy-start(bf16[64,1792]{1,0:T(8,128)(2,1)} %param.9) | copy-start | bytes 688132
  42.1 82.8 %copy-start.2 = (bf16[64,1792]{1,0:T(8,128)(2,1)S(1)}, bf16[64,1792]{1,0:T(8,128)(2,1)}, u32[]{:S(2)}) copy-start(bf16[64,1792]{1,0:T(8,128)(2,1)} %param.10) | copy-start | bytes 688132
  42.1 134.6 %all-gather.8.cloned.1.call-start = ((), (), s32[]{:S(2)}) async-start(), calls=%async_computation.4 | async-start | bytes 3899392 | tf_op jit(solution)/shard_map/all_gather | solution.py:29
  127.0 101.3 %all-gather.10.cloned.1.call-start = ((), (), s32[]{:S(2)}) async-start(), calls=%async_computation.5 | async-start | bytes 3899392 | tf_op jit(solution)/shard_map/all_gather | solution.py:30
  127.6 125.2 %all-gather.12.cloned.1.call-start = ((), (), s32[]{:S(2)}) async-start(), calls=%async_computation.7 | async-start | bytes 1179648 | tf_op jit(solution)/shard_map/all_gather | solution.py:21
  128.2 176.3 %all-gather.14.cloned.1.call-start = ((), (), s32[]{:S(2)}) async-start(), calls=%async_computation.8 | async-start | bytes 3899392 | tf_op jit(solution)/shard_map/all_gather | solution.py:16
  128.8 211.9 %reduce-scatter.5.cloned.1.call-start = ((), (), s32[]{:S(2)}) async-start(), calls=%async_computation.6 | async-start | bytes 2359296 | tf_op jit(solution)/shard_map/reduce_scatter | solution.py:32
  259.1 5.2 %copy-start.4 = (bf16[1024,512]{1,0:T(8,128)(2,1)S(1)}, bf16[1024,512]{1,0:T(8,128)(2,1)}, u32[]{:S(2)}) copy-start(bf16[1024,512]{1,0:T(8,128)(2,1)} %all-gather.12.cloned.1.call-done) | copy-start | bytes 3145732
  270.4 34.1 %copy-start.3 = (bf16[1024,512]{1,0:T(8,128)(2,1)S(1)}, bf16[1024,512]{1,0:T(8,128)(2,1)}, u32[]{:S(2)}) copy-start(bf16[1024,512]{1,0:T(8,128)(2,1)} %all-gather.6.cloned.1.call-done) | copy-start | bytes 3145732
Sparse Core Ops, SparseCore 0:
  9.7 26.0 all-gather.5
  42.2 82.6 reduce-scatter.2
  127.9 48.8 all-gather.7
  179.5 48.7 all-gather.9
  230.0 22.7 all-gather.11
  255.1 49.4 all-gather.13
  307.6 32.9 reduce-scatter.4

commit v2 on v1

v2 whole, which is shorter than its diff:
```python
import jax
import jax.numpy as jnp
from jax import lax
from jax.experimental import pallas as pl
from jax.experimental.pallas import tpu as pltpu
from jax.sharding import PartitionSpec as P

MESH = pl.DeviceIdType.MESH
F32 = jnp.float32
BF16 = jnp.bfloat16
NT = (((1,), (1,)), ((), ()))
TN = (((0,), (0,)), ((), ()))
N = 4
ROWS = 16
D = 512
F = 1792
HALF = F // 2
TILE = 256


def _exchange(
    og_ref, in_ref, gate_ref, up_ref, gw_hbm, uw_hbm, dw_hbm,
    ig_ref, all_hbm, in_hbm, og_hbm,
    dw, gw, uw, og_all, in_all, arr, part, sb, ra, vf, rb, ip, ri, rz,
    load_sem, store_sem, og_s, og_r, in_s, in_r, rs_s, rs_r, ag_s, ag_r, ig_s, ig_r,
):
    row, col = lax.axis_index("row"), lax.axis_index("col")
    y, x = row // N, row % N
    z, k = col // 2, col % 2

    def at(base, step):
        return (base + (step + N)) % N

    def chip(axis, step):
        if axis == "y":
            return (at(y, step) * N + x, col)
        return (y * N + at(x, step), col)

    def column(step):
        return (row, (col + step) % 8)

    axes = (("y", "x"), ("x", "y"))
    place = ((y, x), (x, y))
    cols = (pl.ds(0, HALF), pl.ds(HALF, HALF))

    barrier = pltpu.get_barrier_semaphore()
    for axis in ("y", "x"):
        for step in (1, -1):
            pl.semaphore_signal(barrier, inc=1, device_id=chip(axis, step), device_id_type=MESH)
    for step in range(1, 8):
        pl.semaphore_signal(barrier, inc=1, device_id=column(step), device_id_type=MESH)

    loads = [
        pltpu.make_async_copy(dw_hbm, dw, load_sem.at[0]),
        pltpu.make_async_copy(gw_hbm, gw, load_sem.at[1]),
        pltpu.make_async_copy(uw_hbm, uw, load_sem.at[2]),
    ]
    for load in loads:
        load.start()

    for j in range(N):
        for half in range(2):
            own = pl.ds(half * N * ROWS + j * ROWS, ROWS)
            og_all[j, 2 * col + half] = og_ref[own, :]
            in_all[j, 2 * col + half] = in_ref[own, :]

    def remote(src, dst, ssem, rsem, device):
        return pltpu.make_async_remote_copy(
            src_ref=src, dst_ref=dst, send_sem=ssem, recv_sem=rsem,
            device_id=device, device_id_type=MESH,
        )

    def og_copy(j, step, origin):
        block = og_all.at[j, pl.ds(2 * origin, 2)]
        return remote(block, block, og_s.at[j, step - 1], og_r.at[j, step - 1], column(step))

    def in_copy(step, origin):
        block = in_all.at[:, pl.ds(2 * origin, 2)]
        return remote(block, block, in_s.at[step - 1], in_r.at[step - 1], column(step))

    def slots(v):
        return jnp.maximum(2 + 2 * v, 0)

    def item(v):
        return jnp.maximum(1 + v, 0)

    def block(s, first, count, b):
        a = place[s][0]
        if s == 0:
            return arr.at[pl.ds(first, count), a, b, :, cols[s]]
        return arr.at[pl.ds(first, count), b, a, :, cols[s]]

    def group(s, first, count, a):
        if s == 0:
            return arr.at[pl.ds(first, count), a, :, :, cols[s]]
        return arr.at[pl.ds(first, count), :, a, :, cols[s]]

    def ag(kind, v, s, sending):
        a, b = place[s]
        first = slots(v)
        step = 1 if kind % 2 == 0 else -1
        axis = axes[s][1] if kind < 4 else axes[s][0]
        here = b if kind < 4 else a
        if kind in (0, 1, 4, 5):
            lead, count = first, 2
            origin = here if sending else at(here, -step)
        else:
            lead, count = first + (0 if step == 1 else 1), 1
            origin = at(here, -step) if sending else at(here, 2)
        view = block(s, lead, count, origin) if kind < 4 else group(s, lead, count, origin)
        return remote(
            view, view, ag_s.at[kind, item(v), s], ag_r.at[kind, item(v), s], chip(axis, step)
        )

    def ag_a0(v):
        for s in range(2):
            ag(0, v, s, True).start()
            ag(1, v, s, True).start()

    def ag_a1(v):
        for s in range(2):
            for kind in (0, 1):
                ag(kind, v, s, False).wait_recv()
                ag(kind + 2, v, s, True).start()

    def ag_a2(v):
        for s in range(2):
            ag(2, v, s, False).wait_recv()
            ag(3, v, s, False).wait_recv()
            ag(4, v, s, True).start()
            ag(5, v, s, True).start()

    def ag_a3(v):
        for s in range(2):
            for kind in (4, 5):
                ag(kind, v, s, False).wait_recv()
                ag(kind + 2, v, s, True).start()

    def store(v):
        two = pl.ds(slots(v), 2)
        return pltpu.make_async_copy(arr.at[two], all_hbm.at[two], store_sem.at[item(v)])

    def ag_a4(v):
        for s in range(2):
            ag(6, v, s, False).wait_recv()
            ag(7, v, s, False).wait_recv()
        store(v).start()

    def rs(kind, j, s, o, sending):
        step = 1 if o == 0 else -1
        a, b = place[s]
        number = kind % 3
        direction = -step if number == 2 else step
        ssem, rsem = rs_s.at[kind, j, s, o], rs_r.at[kind, j, s, o]
        if kind < 3:
            two = pl.ds(2 * o, 2)
            src = sb.at[number, j, s, two]
            dst = ra.at[number, j, s, two]
            device = chip(axes[s][0], direction)
        else:
            eight = pl.ds(8 * o, 8)
            target = (at(b, 2), at(b, step), at(b, -step))[number]
            src = vf.at[j, s, target, eight]
            dst = rb.at[number, j, s, eight]
            device = chip(axes[s][1], direction)
        return remote(src, dst, ssem, rsem, device)

    def own_part(j, s, a, o):
        two = pl.ds(2 * o, 2)
        if s == 0:
            return part[j, a, two, :, cols[s]]
        return part[j, two, a, :, cols[s]]

    def rs_s0(j):
        for step in range(1, 8):
            og_copy(j, step, (col + 8 - step) % 8).wait_recv()
        lhs = og_all[j].reshape(16 * ROWS, D)

        @pl.loop(0, F // TILE)
        def _(n):
            at_n = pl.ds(pl.multiple_of(n * TILE, TILE), TILE)
            out = lax.dot_general(lhs, dw[at_n, :], NT, preferred_element_type=F32)
            part[j, :, :, :, at_n] = out.reshape(N, N, ROWS, TILE)

        for s in range(2):
            a = place[s][0]
            for o in range(2):
                step = 1 if o == 0 else -1
                two = pl.ds(2 * o, 2)
                sb[0, j, s, two] = own_part(j, s, at(a, 2), o).astype(BF16)
                rs(0, j, s, o, True).start()
        for s in range(2):
            a = place[s][0]
            for o in range(2):
                step = 1 if o == 0 else -1
                two = pl.ds(2 * o, 2)
                sb[2, j, s, two] = own_part(j, s, at(a, -step), o).astype(BF16)
                rs(2, j, s, o, True).start()

    def rs_s1(j):
        for s in range(2):
            a = place[s][0]
            for o in range(2):
                step = 1 if o == 0 else -1
                two = pl.ds(2 * o, 2)
                rs(0, j, s, o, False).wait_recv()
                total = own_part(j, s, at(a, step), o) + ra[0, j, s, two].astype(F32)
                sb[1, j, s, two] = total.astype(BF16)
                rs(1, j, s, o, True).start()

    def rs_s2(j):
        for s in range(2):
            a = place[s][0]
            for o in range(2):
                two = pl.ds(2 * o, 2)
                rs(2, j, s, o, False).wait_recv()
                rs(1, j, s, o, False).wait_recv()
                vf[j, s, two] = (
                    own_part(j, s, a, o)
                    + ra[1, j, s, two].astype(F32)
                    + ra[2, j, s, two].astype(F32)
                )
            for o in range(2):
                rs(3, j, s, o, True).start()
                rs(5, j, s, o, True).start()

    def rs_s3(j):
        for s in range(2):
            b = place[s][1]
            for o in range(2):
                step = 1 if o == 0 else -1
                eight = pl.ds(8 * o, 8)
                rs(3, j, s, o, False).wait_recv()
                vf[j, s, at(b, step), eight] = vf[j, s, at(b, step), eight] + rb[0, j, s, eight]
                rs(4, j, s, o, True).start()

    def pre(j, s):
        own = pl.ds(pl.multiple_of(j * ROWS, ROWS), ROWS)
        gate = gate_ref[own, cols[s]].astype(F32)
        up = up_ref[own, cols[s]].astype(F32)
        return gate, up, 1.0 / (1.0 + jnp.exp(-gate))

    def rs_s4(j):
        for s in range(2):
            b = place[s][1]
            for o in range(2):
                rs(5, j, s, o, False).wait_recv()
                rs(4, j, s, o, False).wait_recv()
            grad = vf[j, s, b] + rb[1, j, s] + rb[2, j, s]
            gate, up, sig = pre(j, s)
            first = slots(j)
            arr[first, y, x, :, cols[s]] = (grad * up * sig * (1.0 + gate * (1.0 - sig))).astype(BF16)
            arr[first + 1, y, x, :, cols[s]] = (grad * gate * sig).astype(BF16)
            ag(0, j, s, True).start()
            ag(1, j, s, True).start()

    def hidden(slot, j):
        for s in range(2):
            gate, up, sig = pre(j, s)
            arr[slot, y, x, :, cols[s]] = (gate * sig * up).astype(BF16)

    def ig_pair(j):
        return remote(ip.at[j, :, 1 - k], ri.at[j], ig_s.at[0, j], ig_r.at[0, j], (row, 2 * z + 1 - k))

    def ig_send(j, step):
        return remote(
            ip.at[j, at(z, step), k], rz.at[j, step - 1],
            ig_s.at[step, j], ig_r.at[step, j], (row, 2 * at(z, step) + k),
        )

    def ig_i0(j):
        first = slots(j)
        for n in range(D // TILE):
            at_n = pl.ds(n * TILE, TILE)
            out = lax.dot_general(
                arr[first].reshape(16 * ROWS, F), gw[at_n, :], NT, preferred_element_type=F32
            ) + lax.dot_general(
                arr[first + 1].reshape(16 * ROWS, F), uw[at_n, :], NT, preferred_element_type=F32
            )
            ip[j, :, :, :, :, at_n] = out.reshape(N, 2, 2, ROWS, TILE)
        ig_pair(j).start()

    def ig_i1(j):
        ig_pair(j).wait_recv()
        for step in (2, 1, 3, 0):
            t = at(z, step)
            ip[j, t, k] = ip[j, t, k] + ri[j, t]
            if step:
                ig_send(j, step).start()

    def ig_i2(j):
        for step in (1, 2, 3):
            ig_send(j, step).wait_recv()
        total = ip[j, z, k] + rz[j, 0] + rz[j, 1] + rz[j, 2]
        for half in range(2):
            own = pl.ds(pl.multiple_of(half * N * ROWS + j * ROWS, ROWS), ROWS)
            ig_ref[own, :] = total[half]

    pl.semaphore_wait(barrier, 11)
    for j in range(N):
        for step in (4, 3, 5, 2, 6, 1, 7):
            og_copy(j, step, col).start()
    hidden(0, 0)
    hidden(1, 1)
    ag_a0(-6)
    for step in (4, 3, 5, 2, 6, 1, 7):
        in_copy(step, col).start()
    hidden(10, 2)
    hidden(11, 3)
    ag_a0(4)
    ag_a1(-6)
    ag_a2(-6)
    loads[0].wait()

    def stage(t, number, count, call):
        j = t - number

        @pl.when((j >= 0) & (j < count))
        def _():
            call(j)

    @pl.loop(0, 14)
    def _(t):
        stage(t, 4, N, rs_s4)
        stage(t, 3, N, rs_s3)
        stage(t, 2, N, rs_s2)
        stage(t, 1, N, rs_s1)
        stage(t, 0, N, rs_s0)

        @pl.when(t == 1)
        def _():
            ag_a3(-6)

        @pl.when(t == 7)
        def _():
            loads[1].wait()
            loads[2].wait()

        stage(t, 5, N + 1, ag_a1)
        stage(t, 6, N + 1, ag_a2)
        stage(t, 7, N + 1, ag_a3)
        stage(t, 9, N, ig_i1)
        stage(t, 8, N, ag_a4)
        stage(t, 8, N, ig_i0)
        stage(t, 10, N, ig_i2)

        @pl.when(t == 6)
        def _():
            ag_a4(-6)

        @pl.when(t == 9)
        def _():
            for step in range(1, 8):
                in_copy(step, (col + 8 - step) % 8).wait_recv()
            pltpu.make_async_copy(in_all, in_hbm, store_sem.at[6]).start()
            pltpu.make_async_copy(og_all, og_hbm, store_sem.at[7]).start()

    ag_a4(4)
    for j in range(N):
        for step in range(1, 8):
            og_copy(j, step, col).wait_send()
    for step in range(1, 8):
        in_copy(step, col).wait_send()

    @pl.loop(0, N)
    def _(j):
        for s in range(2):
            for o in range(2):
                for kind in range(6):
                    rs(kind, j, s, o, True).wait_send()
        ig_pair(j).wait_send()
        for step in (1, 2, 3):
            ig_send(j, step).wait_send()

    @pl.loop(0, 6)
    def _(i):
        for s in range(2):
            for kind in range(8):
                ag(kind, i - 1, s, True).wait_send()
        store(i - 1).wait()

    pltpu.make_async_copy(in_all, in_hbm, store_sem.at[6]).wait()
    pltpu.make_async_copy(og_all, og_hbm, store_sem.at[7]).wait()


def exchange(out_grad, inputs, gate_pre, up_pre, gate_weight, up_weight, down_weight):
    vmem = pl.BlockSpec(memory_space=pltpu.VMEM)
    hbm = pl.BlockSpec(memory_space=pl.ANY)
    dma = pltpu.SemaphoreType.DMA
    return pl.pallas_call(
        _exchange,
        out_shape=(
            jax.ShapeDtypeStruct((128, D), F32),
            jax.ShapeDtypeStruct((12, N, N, ROWS, F), BF16),
            jax.ShapeDtypeStruct((N, 16, ROWS, D), BF16),
            jax.ShapeDtypeStruct((N, 16, ROWS, D), BF16),
        ),
        in_specs=[vmem] * 4 + [hbm] * 3,
        out_specs=(vmem, hbm, hbm, hbm),
        scratch_shapes=[
            pltpu.VMEM((F, D), BF16),
            pltpu.VMEM((D, F), BF16),
            pltpu.VMEM((D, F), BF16),
            pltpu.VMEM((N, 16, ROWS, D), BF16),
            pltpu.VMEM((N, 16, ROWS, D), BF16),
            pltpu.VMEM((12, N, N, ROWS, F), BF16),
            pltpu.VMEM((N, N, N, ROWS, F), F32),
            pltpu.VMEM((3, N, 2, N, ROWS, HALF), BF16),
            pltpu.VMEM((3, N, 2, N, ROWS, HALF), BF16),
            pltpu.VMEM((N, 2, N, ROWS, HALF), F32),
            pltpu.VMEM((3, N, 2, ROWS, HALF), F32),
            pltpu.VMEM((N, N, 2, 2, ROWS, D), F32),
            pltpu.VMEM((N, N, 2, ROWS, D), F32),
            pltpu.VMEM((N, 3, 2, ROWS, D), F32),
            dma((3,)),
            dma((8,)),
            dma((N, 7)),
            dma((N, 7)),
            dma((7,)),
            dma((7,)),
            dma((6, N, 2, 2)),
            dma((6, N, 2, 2)),
            dma((8, 6, 2)),
            dma((8, 6, 2)),
            dma((4, N)),
            dma((4, N)),
        ],
        compiler_params=pltpu.CompilerParams(
            collective_id=0, has_side_effects=True, vmem_limit_bytes=58 << 20
        ),
        cost_estimate=pl.CostEstimate(
            flops=6 * 1024 * D * F, bytes_accessed=20 << 20, transcendentals=64 * F
        ),
        name="exchange",
    )(out_grad, inputs, gate_pre, up_pre, gate_weight, up_weight, down_weight)


def _weights(arr_ref, in_ref, og_ref, gg_ref, ug_ref, dg_ref):
    def tokens(numbers):
        return jnp.concatenate([arr_ref[n] for n in numbers], axis=0)

    inputs, out_grad = in_ref[...], og_ref[...]
    gg_ref[...] = lax.dot_general(inputs, tokens((2, 4, 6, 8)), TN, preferred_element_type=F32)
    ug_ref[...] = lax.dot_general(inputs, tokens((3, 5, 7, 9)), TN, preferred_element_type=F32)
    dg_ref[...] = lax.dot_general(tokens((0, 1, 10, 11)), out_grad, TN, preferred_element_type=F32)


def weights(arr, inputs, out_grad):
    return pl.pallas_call(
        _weights,
        grid=(F // TILE,),
        out_shape=(
            jax.ShapeDtypeStruct((D, F), F32),
            jax.ShapeDtypeStruct((D, F), F32),
            jax.ShapeDtypeStruct((F, D), F32),
        ),
        in_specs=[
            pl.BlockSpec((12, 256, TILE), lambda n: (0, 0, n)),
            pl.BlockSpec((1024, D), lambda n: (0, 0)),
            pl.BlockSpec((1024, D), lambda n: (0, 0)),
        ],
        out_specs=(
            pl.BlockSpec((D, TILE), lambda n: (0, n)),
            pl.BlockSpec((D, TILE), lambda n: (0, n)),
            pl.BlockSpec((TILE, D), lambda n: (n, 0)),
        ),
        compiler_params=pltpu.CompilerParams(vmem_limit_bytes=40 << 20),
        name="weights",
    )(arr, inputs, out_grad)


def body(inputs, out_grad, gate_pre, up_pre, gate_weight, up_weight, down_weight):
    input_grad, arr, in_all, og_all = exchange(
        out_grad, inputs, gate_pre, up_pre, gate_weight, up_weight, down_weight
    )
    gate_grad, up_grad, down_grad = weights(
        arr.reshape(12, 256, F), in_all.reshape(1024, D), og_all.reshape(1024, D)
    )
    return (input_grad, gate_grad, up_grad, down_grad)


def solution(mesh):
    in_specs = (
        P("col", "row"),
        P("col", "row"),
        P("row", "col"),
        P("row", "col"),
        P("row", "col"),
        P("row", "col"),
        P("col", "row"),
    )
    out_specs = (P("col", "row"), P("row", "col"), P("row", "col"), P("col", "row"))
    return jax.shard_map(body, mesh=mesh, in_specs=in_specs, out_specs=out_specs, check_vma=False)
```

time: 348 us -> 122 us (0.35)
  waiting for transfers between devices: 283 us -> 0 us
  Pallas kernels: 0 us -> 112 us
  matrix products: 37.4 us -> 0 us
  between operations: 14.1 us -> 0.65 us
    all_gather x5 -> x0, waiting for transfers between devices: 168 us -> none  [the longest x1 47.9 us: body(): gate_all = lax.all_gather(grad_gate, 'row', axis=0, tiled=True)]
    reduce_scatter x2 -> x0, waiting for transfers between devices: 113 us -> none  [the longest x1 82.8 us: body(): lax.psum_scatter(partial_sum, 'row', scatter_dimension=0, tiled=True)]
    pallas_call x0 -> x2, Pallas kernels: none -> 112 us  [the longest x1 103 us: exchange(): pl.pallas_call(_exchange, out_shape=(jax.ShapeDtypeStruct((128, D), F32),...]
    dot_general x6 -> x0, matrix products: 37.4 us -> none  [the longest x1 6.74 us: body(): lax.dot_general(up_all, up_weight, LAST_DIMS, preferred_element_type=jnp....]
    unnamed x12 -> x9, local copies, waits for them, and re-layouts: 10.5 us -> 7.28 us
  transfers between devices with their start and end apart: 7 -> 0, of which waited for: 7 -> 0; matrix products, arithmetic and copies ran while one was open for 12% -> 0% of each run, Pallas kernels for 0% -> 0%
where the time goes in v2:
time: 122 us; the launch traced here: 120 us
  Pallas kernels  112 us (92%)
  local copies, waits for them, and re-layouts  7.28 us (6%)
    pallas_call x1, Pallas kernels, exchange(): pl.pallas_call(_exchange, out_shape=(jax.ShapeDtypeStruct((128, D), F32),...  103 us
    pallas_call x1, Pallas kernels, weights(): pl.pallas_call(_weights, grid=(F // TILE,), out_shape=(jax.ShapeDtypeStru...  8.75 us
    unnamed x9, local copies, waits for them, and re-layouts  7.28 us

profile of v2, /device:TPU:0, one launch (start us, length us, event | category | flops | bytes accessed | tf_op | source)
XLA Modules:
  0.0 120.1 jit_solution(3099293027068649695)
XLA Ops:
  0.6 103.4 %exchange.1 = (f32[128,512]{1,0:T(8,128)}, bf16[12,4,4,16,1792]{4,3,2,1,0:T(8,128)(2,1)}, bf16[4,16,16,512]{3,2,1,0:T(8,128)(2,1)}, bf16[4,16,16,512]{3,2,1,0:T(8,128)(2,1)}) custom-call(bf16[128,512]{1,0:T(8,128)(2,1)} %og_ref.1, bf16[128,512]{1,0:T(8,128)(2,1)} %in_ref.1, bf16[64,1792]{1,0:T(8,128)(2,1)} %gate_ref.1, bf16[64,1792]{1,0:T(8,128)(2,1)} %up_ref.1, ...), custom_call_target="tpu_custom_call" | custom-call | flops 5637144576 | bytes 20971520 | tf_op jit(solution)/shard_map/exchange/pallas_call | solution.py:390
  104.1 0.0 copy-start
  104.1 4.1 %copy-done = bf16[12,4,4,16,1792]{4,3,2,1,0:T(8,128)(2,1)S(1)} copy-done((bf16[12,4,4,16,1792]{4,3,2,1,0:T(8,128)(2,1)S(1)}, bf16[12,4,4,16,1792]{4,3,2,1,0:T(8,128)(2,1)}, u32[]{:S(2)}) %copy-start) | copy-done | bytes 11010072
  108.2 0.0 copy-start.1
  108.2 1.2 %copy-done.1 = bf16[4,16,16,512]{3,2,1,0:T(8,128)(2,1)S(1)} copy-done((bf16[4,16,16,512]{3,2,1,0:T(8,128)(2,1)S(1)}, bf16[4,16,16,512]{3,2,1,0:T(8,128)(2,1)}, u32[]{:S(2)}) %copy-start.1) | copy-done | bytes 1048600
  109.4 0.0 copy-start.2
  109.4 1.2 %copy-done.2 = bf16[4,16,16,512]{3,2,1,0:T(8,128)(2,1)S(1)} copy-done((bf16[4,16,16,512]{3,2,1,0:T(8,128)(2,1)S(1)}, bf16[4,16,16,512]{3,2,1,0:T(8,128)(2,1)}, u32[]{:S(2)}) %copy-start.2) | copy-done | bytes 1048600
  110.6 0.0 copy-start.3
  110.6 8.7 %weights.1 = (f32[512,1792]{1,0:T(8,128)}, f32[512,1792]{1,0:T(8,128)}, f32[1792,512]{1,0:T(8,128)}) custom-call(bf16[12,256,1792]{2,1,0:T(8,128)(2,1)S(1)} %bitcast.3, bf16[1024,512]{1,0:T(8,128)(2,1)S(1)} %bitcast.4, bf16[1024,512]{1,0:T(8,128)(2,1)S(1)} %bitcast.5), custom_call_target="tpu_custom_call" | custom-call | tf_op jit(solution)/shard_map/weights/pallas_call | solution.py:449
  119.4 0.0 copy-done.3
  119.4 0.7 copy.12
Async XLA Ops:
  104.1 4.1 %copy-start = (bf16[12,4,4,16,1792]{4,3,2,1,0:T(8,128)(2,1)S(1)}, bf16[12,4,4,16,1792]{4,3,2,1,0:T(8,128)(2,1)}, u32[]{:S(2)}) copy-start(bf16[12,4,4,16,1792]{4,3,2,1,0:T(8,128)(2,1)} %get-tuple-element.12) | copy-start | bytes 33030148
  108.2 1.2 %copy-start.1 = (bf16[4,16,16,512]{3,2,1,0:T(8,128)(2,1)S(1)}, bf16[4,16,16,512]{3,2,1,0:T(8,128)(2,1)}, u32[]{:S(2)}) copy-start(bf16[4,16,16,512]{3,2,1,0:T(8,128)(2,1)} %get-tuple-element.13) | copy-start | bytes 3145732
  109.4 1.2 %copy-start.2 = (bf16[4,16,16,512]{3,2,1,0:T(8,128)(2,1)S(1)}, bf16[4,16,16,512]{3,2,1,0:T(8,128)(2,1)}, u32[]{:S(2)}) copy-start(bf16[4,16,16,512]{3,2,1,0:T(8,128)(2,1)} %get-tuple-element.14) | copy-start | bytes 3145732
  110.6 8.8 %copy-start.3 = (f32[128,512]{1,0:T(8,128)S(1)}, f32[128,512]{1,0:T(8,128)}, u32[]{:S(2)}) copy-start(f32[128,512]{1,0:T(8,128)} %get-tuple-element.22) | copy-start | bytes 786436

commit v3 on v2

--- a/solution.py
+++ b/solution.py
@@ -20,9 +20,9 @@
 
 def _exchange(
     og_ref, in_ref, gate_ref, up_ref, gw_hbm, uw_hbm, dw_hbm,
-    ig_ref, all_hbm, in_hbm, og_hbm,
-    dw, gw, uw, og_all, in_all, arr, part, sb, ra, vf, rb, ip, ri, rz,
-    load_sem, store_sem, og_s, og_r, in_s, in_r, rs_s, rs_r, ag_s, ag_r, ig_s, ig_r,
+    ig_ref, gg_ref, ug_ref, dg_ref,
+    dw, gw, uw, og_all, in_all, in_t, arr, part, sb, ra, vf, rb, ip, ri, rz,
+    load_sem, og_s, og_r, in_s, in_r, rs_s, rs_r, ag_s, ag_r, ig_s, ig_r,
 ):
     row, col = lax.axis_index("row"), lax.axis_index("col")
     y, x = row // N, row % N
@@ -79,10 +79,10 @@
         return remote(block, block, in_s.at[step - 1], in_r.at[step - 1], column(step))
 
     def slots(v):
-        return jnp.maximum(2 + 2 * v, 0)
+        return jnp.clip(2 + 2 * v, 0, 10)
 
     def item(v):
-        return jnp.maximum(1 + v, 0)
+        return jnp.clip(1 + v, 0, 5)
 
     def block(s, first, count, b):
         a = place[s][0]
@@ -136,15 +136,10 @@
                 ag(kind, v, s, False).wait_recv()
                 ag(kind + 2, v, s, True).start()
 
-    def store(v):
-        two = pl.ds(slots(v), 2)
-        return pltpu.make_async_copy(arr.at[two], all_hbm.at[two], store_sem.at[item(v)])
-
     def ag_a4(v):
         for s in range(2):
             ag(6, v, s, False).wait_recv()
             ag(7, v, s, False).wait_recv()
-        store(v).start()
 
     def rs(kind, j, s, o, sending):
         step = 1 if o == 0 else -1
@@ -296,6 +291,36 @@
             own = pl.ds(pl.multiple_of(half * N * ROWS + j * ROWS, ROWS), ROWS)
             ig_ref[own, :] = total[half]
 
+    def wg(j):
+        first = slots(j)
+        for ref, slot in ((gg_ref, first), (ug_ref, first + 1)):
+
+            @pl.loop(0, F // TILE)
+            def _(n):
+                at_n = pl.ds(pl.multiple_of(n * TILE, TILE), TILE)
+                rhs = arr[slot, :, :, :, at_n].reshape(16 * ROWS, TILE)
+                out = jnp.dot(in_t[j], rhs, preferred_element_type=F32)
+
+                @pl.when(j == 0)
+                def _():
+                    ref[:, at_n] = out
+
+                @pl.when(j > 0)
+                def _():
+                    ref[:, at_n] = ref[:, at_n] + out
+
+    def dg(slot, j, fresh):
+        @pl.loop(0, F // TILE)
+        def _(n):
+            at_n = pl.ds(pl.multiple_of(n * TILE, TILE), TILE)
+            out = ref_dot(slot, j, at_n) + ref_dot(slot + 1, j + 1, at_n)
+            dg_ref[at_n, :] = out if fresh else dg_ref[at_n, :] + out
+
+    def ref_dot(slot, j, at_n):
+        lhs = arr[slot, :, :, :, at_n].reshape(16 * ROWS, TILE)
+        rhs = og_all[j].reshape(16 * ROWS, D)
+        return lax.dot_general(lhs, rhs, TN, preferred_element_type=F32)
+
     pl.semaphore_wait(barrier, 11)
     for j in range(N):
         for step in (4, 3, 5, 2, 6, 1, 7):
@@ -319,6 +344,13 @@
         def _():
             call(j)
 
+    def ag_stage(t, number, call):
+        v = t - number
+
+        @pl.when(((v >= 0) & (v < N)) | (v == N + 1))
+        def _():
+            call(v)
+
     @pl.loop(0, 14)
     def _(t):
         stage(t, 4, N, rs_s4)
@@ -336,10 +368,11 @@
             loads[1].wait()
             loads[2].wait()
 
-        stage(t, 5, N + 1, ag_a1)
-        stage(t, 6, N + 1, ag_a2)
-        stage(t, 7, N + 1, ag_a3)
+        ag_stage(t, 5, ag_a1)
+        ag_stage(t, 6, ag_a2)
+        ag_stage(t, 7, ag_a3)
         stage(t, 9, N, ig_i1)
+        stage(t, 9, N, wg)
         stage(t, 8, N, ag_a4)
         stage(t, 8, N, ig_i0)
         stage(t, 10, N, ig_i2)
@@ -347,15 +380,17 @@
         @pl.when(t == 6)
         def _():
             ag_a4(-6)
-
-        @pl.when(t == 9)
+            dg(0, 0, True)
+
+        @pl.when(t == 7)
         def _():
             for step in range(1, 8):
                 in_copy(step, (col + 8 - step) % 8).wait_recv()
-            pltpu.make_async_copy(in_all, in_hbm, store_sem.at[6]).start()
-            pltpu.make_async_copy(og_all, og_hbm, store_sem.at[7]).start()
+            for j in range(N):
+                in_t[j] = in_all[j].reshape(16 * ROWS, D).T
 
     ag_a4(4)
+    dg(10, 2, False)
     for j in range(N):
         for step in range(1, 8):
             og_copy(j, step, col).wait_send()
@@ -377,10 +412,6 @@
         for s in range(2):
             for kind in range(8):
                 ag(kind, i - 1, s, True).wait_send()
-        store(i - 1).wait()
-
-    pltpu.make_async_copy(in_all, in_hbm, store_sem.at[6]).wait()
-    pltpu.make_async_copy(og_all, og_hbm, store_sem.at[7]).wait()
 
 
 def exchange(out_grad, inputs, gate_pre, up_pre, gate_weight, up_weight, down_weight):
@@ -390,19 +421,20 @@
     return pl.pallas_call(
         _exchange,
         out_shape=(
-            jax.ShapeDtypeStruct((128, D), F32),
-            jax.ShapeDtypeStruct((12, N, N, ROWS, F), BF16),
-            jax.ShapeDtypeStruct((N, 16, ROWS, D), BF16),
-            jax.ShapeDtypeStruct((N, 16, ROWS, D), BF16),
+            pltpu.VMEM((128, D), F32),
+            pltpu.VMEM((D, F), F32),
+            pltpu.VMEM((D, F), F32),
+            pltpu.VMEM((F, D), F32),
         ),
         in_specs=[vmem] * 4 + [hbm] * 3,
-        out_specs=(vmem, hbm, hbm, hbm),
+        out_specs=(vmem, vmem, vmem, vmem),
         scratch_shapes=[
             pltpu.VMEM((F, D), BF16),
             pltpu.VMEM((D, F), BF16),
             pltpu.VMEM((D, F), BF16),
             pltpu.VMEM((N, 16, ROWS, D), BF16),
             pltpu.VMEM((N, 16, ROWS, D), BF16),
+            pltpu.VMEM((N, D, 16 * ROWS), BF16),
             pltpu.VMEM((12, N, N, ROWS, F), BF16),
             pltpu.VMEM((N, N, N, ROWS, F), F32),
             pltpu.VMEM((3, N, 2, N, ROWS, HALF), BF16),
@@ -413,7 +445,6 @@
             pltpu.VMEM((N, N, 2, ROWS, D), F32),
             pltpu.VMEM((N, 3, 2, ROWS, D), F32),
             dma((3,)),
-            dma((8,)),
             dma((N, 7)),
             dma((N, 7)),
             dma((7,)),
@@ -426,7 +457,7 @@
             dma((4, N)),
         ],
         compiler_params=pltpu.CompilerParams(
-            collective_id=0, has_side_effects=True, vmem_limit_bytes=58 << 20
+            collective_id=0, has_side_effects=True, vmem_limit_bytes=51 << 20
         ),
         cost_estimate=pl.CostEstimate(
             flops=6 * 1024 * D * F, bytes_accessed=20 << 20, transcendentals=64 * F
@@ -435,48 +466,32 @@
     )(out_grad, inputs, gate_pre, up_pre, gate_weight, up_weight, down_weight)
 
 
-def _weights(arr_ref, in_ref, og_ref, gg_ref, ug_ref, dg_ref):
-    def tokens(numbers):
-        return jnp.concatenate([arr_ref[n] for n in numbers], axis=0)
-
-    inputs, out_grad = in_ref[...], og_ref[...]
-    gg_ref[...] = lax.dot_general(inputs, tokens((2, 4, 6, 8)), TN, preferred_element_type=F32)
-    ug_ref[...] = lax.dot_general(inputs, tokens((3, 5, 7, 9)), TN, preferred_element_type=F32)
-    dg_ref[...] = lax.dot_general(tokens((0, 1, 10, 11)), out_grad, TN, preferred_element_type=F32)
-
-
-def weights(arr, inputs, out_grad):
+def _write(a, b, c, d, a_out, b_out, c_out, d_out, sem):
+    copies = []
+    for i, (src, dst) in enumerate(((b, b_out), (c, c_out), (d, d_out), (a, a_out))):
+        copies.append(pltpu.make_async_copy(src, dst, sem.at[i]))
+        copies[i].start()
+    for copy in copies:
+        copy.wait()
+
+
+def write(*grads):
+    grads = [pltpu.with_memory_space_constraint(g, pltpu.VMEM) for g in grads]
+    hbm = pl.BlockSpec(memory_space=pl.ANY)
     return pl.pallas_call(
-        _weights,
-        grid=(F // TILE,),
-        out_shape=(
-            jax.ShapeDtypeStruct((D, F), F32),
-            jax.ShapeDtypeStruct((D, F), F32),
-            jax.ShapeDtypeStruct((F, D), F32),
-        ),
-        in_specs=[
-            pl.BlockSpec((12, 256, TILE), lambda n: (0, 0, n)),
-            pl.BlockSpec((1024, D), lambda n: (0, 0)),
-            pl.BlockSpec((1024, D), lambda n: (0, 0)),
-        ],
-        out_specs=(
-            pl.BlockSpec((D, TILE), lambda n: (0, n)),
-            pl.BlockSpec((D, TILE), lambda n: (0, n)),
-            pl.BlockSpec((TILE, D), lambda n: (n, 0)),
-        ),
-        compiler_params=pltpu.CompilerParams(vmem_limit_bytes=40 << 20),
-        name="weights",
-    )(arr, inputs, out_grad)
+        _write,
+        out_shape=[pltpu.HBM(g.shape, g.dtype) for g in grads],
+        in_specs=[pl.BlockSpec(memory_space=pltpu.VMEM)] * 4,
+        out_specs=[hbm] * 4,
+        scratch_shapes=[pltpu.SemaphoreType.DMA((4,))],
+        compiler_params=pltpu.CompilerParams(vmem_limit_bytes=2 << 20),
+        name="write",
+    )(*grads)
 
 
 def body(inputs, out_grad, gate_pre, up_pre, gate_weight, up_weight, down_weight):
-    input_grad, arr, in_all, og_all = exchange(
-        out_grad, inputs, gate_pre, up_pre, gate_weight, up_weight, down_weight
-    )
-    gate_grad, up_grad, down_grad = weights(
-        arr.reshape(12, 256, F), in_all.reshape(1024, D), og_all.reshape(1024, D)
-    )
-    return (input_grad, gate_grad, up_grad, down_grad)
+    grads = exchange(out_grad, inputs, gate_pre, up_pre, gate_weight, up_weight, down_weight)
+    return tuple(write(*grads))
 
 
 def solution(mesh):

time: 122 us -> 113 us (0.926)
  local copies, waits for them, and re-layouts: 7.28 us -> 0 us
    unnamed x9 -> x0, local copies, waits for them, and re-layouts: 7.28 us -> none
where the time goes in v3:
time: 113 us; the launch traced here: 112 us
  Pallas kernels  111 us (98%)
    pallas_call x1, Pallas kernels, exchange(): pl.pallas_call(_exchange, out_shape=(pltpu.VMEM((128, D), F32), pltpu.VME...  107 us
    pallas_call x1, Pallas kernels, write(): pl.pallas_call(_write, out_shape=[pltpu.HBM(g.shape, g.dtype) for g in gr...  4.29 us

profile of v3, /device:TPU:0, one launch (start us, length us, event | category | flops | bytes accessed | tf_op | source)
XLA Modules:
  0.0 111.9 jit_solution(1572400747794259918)
XLA Ops:
  0.6 106.9 %exchange.1 = (f32[128,512]{1,0:T(8,128)S(1)}, f32[512,1792]{1,0:T(8,128)S(1)}, f32[512,1792]{1,0:T(8,128)S(1)}, f32[1792,512]{1,0:T(8,128)S(1)}) custom-call(bf16[128,512]{1,0:T(8,128)(2,1)} %og_ref.1, bf16[128,512]{1,0:T(8,128)(2,1)} %in_ref.1, bf16[64,1792]{1,0:T(8,128)(2,1)} %gate_ref.1, bf16[64,1792]{1,0:T(8,128)(2,1)} %up_ref.1, ...), custom_call_target="tpu_custom_call" | custom-call | flops 5637144576 | bytes 20971520 | tf_op jit(solution)/shard_map/exchange/pallas_call | solution.py:421
  107.6 4.3 %write.1 = (f32[128,512]{1,0:T(8,128)}, f32[512,1792]{1,0:T(8,128)}, f32[512,1792]{1,0:T(8,128)}, f32[1792,512]{1,0:T(8,128)}) custom-call(f32[128,512]{1,0:T(8,128)S(1)} %get-tuple-element.8.a, f32[512,1792]{1,0:T(8,128)S(1)} %get-tuple-element.9.b, f32[512,1792]{1,0:T(8,128)S(1)} %get-tuple-element.10.c, f32[1792,512]{1,0:T(8,128)S(1)} %get-tuple-element.11.d), custom_call_target="tpu_custom_call" | custom-call | tf_op jit(solution)/shard_map/write/pallas_call | solution.py:481

commit v4 on v3

--- a/solution.py
+++ b/solution.py
@@ -19,9 +19,9 @@
 
 
 def _exchange(
-    og_ref, in_ref, gate_ref, up_ref, gw_hbm, uw_hbm, dw_hbm,
-    ig_ref, gg_ref, ug_ref, dg_ref,
-    dw, gw, uw, og_all, in_all, in_t, arr, part, sb, ra, vf, rb, ip, ri, rz,
+    og_hbm, in_hbm, gate_hbm, up_hbm, gw_hbm, uw_hbm, dw_hbm,
+    ig_ref, gg_ref, ug_ref, arr, og_all,
+    og_ref, in_ref, gate_ref, up_ref, dw, gw, uw, in_all, in_t, part, sb, ra, vf, rb, ip, ri, rz,
     load_sem, og_s, og_r, in_s, in_r, rs_s, rs_r, ag_s, ag_r, ig_s, ig_r,
 ):
     row, col = lax.axis_index("row"), lax.axis_index("col")
@@ -51,6 +51,10 @@
         pl.semaphore_signal(barrier, inc=1, device_id=column(step), device_id_type=MESH)
 
     loads = [
+        pltpu.make_async_copy(og_hbm, og_ref, load_sem.at[3]),
+        pltpu.make_async_copy(in_hbm, in_ref, load_sem.at[4]),
+        pltpu.make_async_copy(gate_hbm, gate_ref, load_sem.at[5]),
+        pltpu.make_async_copy(up_hbm, up_ref, load_sem.at[6]),
         pltpu.make_async_copy(dw_hbm, dw, load_sem.at[0]),
         pltpu.make_async_copy(gw_hbm, gw, load_sem.at[1]),
         pltpu.make_async_copy(uw_hbm, uw, load_sem.at[2]),
@@ -58,6 +62,8 @@
     for load in loads:
         load.start()
 
+    loads[0].wait()
+    loads[1].wait()
     for j in range(N):
         for half in range(2):
             own = pl.ds(half * N * ROWS + j * ROWS, ROWS)
@@ -171,7 +177,7 @@
             og_copy(j, step, (col + 8 - step) % 8).wait_recv()
         lhs = og_all[j].reshape(16 * ROWS, D)
 
-        @pl.loop(0, F // TILE)
+        @pl.loop(0, F // TILE, unroll=True)
         def _(n):
             at_n = pl.ds(pl.multiple_of(n * TILE, TILE), TILE)
             out = lax.dot_general(lhs, dw[at_n, :], NT, preferred_element_type=F32)
@@ -301,30 +307,17 @@
                 rhs = arr[slot, :, :, :, at_n].reshape(16 * ROWS, TILE)
                 out = jnp.dot(in_t[j], rhs, preferred_element_type=F32)
 
-                @pl.when(j == 0)
-                def _():
-                    ref[:, at_n] = out
-
-                @pl.when(j > 0)
-                def _():
-                    ref[:, at_n] = ref[:, at_n] + out
-
-    def dg(slot, j, fresh):
-        @pl.loop(0, F // TILE)
-        def _(n):
-            at_n = pl.ds(pl.multiple_of(n * TILE, TILE), TILE)
-            out = ref_dot(slot, j, at_n) + ref_dot(slot + 1, j + 1, at_n)
-            dg_ref[at_n, :] = out if fresh else dg_ref[at_n, :] + out
-
-    def ref_dot(slot, j, at_n):
-        lhs = arr[slot, :, :, :, at_n].reshape(16 * ROWS, TILE)
-        rhs = og_all[j].reshape(16 * ROWS, D)
-        return lax.dot_general(lhs, rhs, TN, preferred_element_type=F32)
+                ref[:, at_n] = jnp.where(j > 0, ref[:, at_n], 0.0) + out
+
+    def turn(j):
+        in_t[j] = in_all[j].reshape(16 * ROWS, D).T
 
     pl.semaphore_wait(barrier, 11)
     for j in range(N):
         for step in (4, 3, 5, 2, 6, 1, 7):
             og_copy(j, step, col).start()
+    loads[2].wait()
+    loads[3].wait()
     hidden(0, 0)
     hidden(1, 1)
     ag_a0(-6)
@@ -334,8 +327,7 @@
     hidden(11, 3)
     ag_a0(4)
     ag_a1(-6)
-    ag_a2(-6)
-    loads[0].wait()
+    loads[4].wait()
 
     def stage(t, number, count, call):
         j = t - number
@@ -350,6 +342,18 @@
         @pl.when(((v >= 0) & (v < N)) | (v == N + 1))
         def _():
             call(v)
+
+    def ag_sent(v):
+        for s in range(2):
+            for kind in range(8):
+                ag(kind, v, s, True).wait_send()
+
+    def sent(j):
+        for s in range(2):
+            for o in range(2):
+                for kind in range(6):
+                    rs(kind, j, s, o, True).wait_send()
+        ag_sent(j)
 
     @pl.loop(0, 14)
     def _(t):
@@ -359,59 +363,56 @@
         stage(t, 1, N, rs_s1)
         stage(t, 0, N, rs_s0)
 
+        @pl.when(t == 0)
+        def _():
+            ag_a2(-6)
+
         @pl.when(t == 1)
         def _():
             ag_a3(-6)
 
         @pl.when(t == 7)
         def _():
-            loads[1].wait()
-            loads[2].wait()
+            loads[5].wait()
+            loads[6].wait()
 
         ag_stage(t, 5, ag_a1)
         ag_stage(t, 6, ag_a2)
         ag_stage(t, 7, ag_a3)
+        @pl.when(t == 7)
+        def _():
+            for step in range(1, 8):
+                in_copy(step, (col + 8 - step) % 8).wait_recv()
+
+        stage(t, 7, N, turn)
+
         stage(t, 9, N, ig_i1)
+        @pl.when(t == 8)
+        def _():
+            ag_a4(-6)
+
         stage(t, 9, N, wg)
+
+        @pl.when(t == 9)
+        def _():
+            for j in range(N):
+                for step in range(1, 8):
+                    og_copy(j, step, col).wait_send()
+            for step in range(1, 8):
+                in_copy(step, col).wait_send()
+            ag_sent(-6)
+
+        stage(t, 10, N, sent)
         stage(t, 8, N, ag_a4)
         stage(t, 8, N, ig_i0)
         stage(t, 10, N, ig_i2)
 
-        @pl.when(t == 6)
-        def _():
-            ag_a4(-6)
-            dg(0, 0, True)
-
-        @pl.when(t == 7)
-        def _():
-            for step in range(1, 8):
-                in_copy(step, (col + 8 - step) % 8).wait_recv()
-            for j in range(N):
-                in_t[j] = in_all[j].reshape(16 * ROWS, D).T
-
     ag_a4(4)
-    dg(10, 2, False)
     for j in range(N):
-        for step in range(1, 8):
-            og_copy(j, step, col).wait_send()
-    for step in range(1, 8):
-        in_copy(step, col).wait_send()
-
-    @pl.loop(0, N)
-    def _(j):
-        for s in range(2):
-            for o in range(2):
-                for kind in range(6):
-                    rs(kind, j, s, o, True).wait_send()
         ig_pair(j).wait_send()
         for step in (1, 2, 3):
             ig_send(j, step).wait_send()
-
-    @pl.loop(0, 6)
-    def _(i):
-        for s in range(2):
-            for kind in range(8):
-                ag(kind, i - 1, s, True).wait_send()
+    ag_sent(4)
 
 
 def exchange(out_grad, inputs, gate_pre, up_pre, gate_weight, up_weight, down_weight):
@@ -424,18 +425,21 @@
             pltpu.VMEM((128, D), F32),
             pltpu.VMEM((D, F), F32),
             pltpu.VMEM((D, F), F32),
-            pltpu.VMEM((F, D), F32),
+            pltpu.VMEM((12, N, N, ROWS, F), BF16),
+            pltpu.VMEM((N, 16, ROWS, D), BF16),
         ),
-        in_specs=[vmem] * 4 + [hbm] * 3,
-        out_specs=(vmem, vmem, vmem, vmem),
+        in_specs=[hbm] * 7,
+        out_specs=(vmem,) * 5,
         scratch_shapes=[
+            pltpu.VMEM((128, D), BF16),
+            pltpu.VMEM((128, D), BF16),
+            pltpu.VMEM((N * ROWS, F), BF16),
+            pltpu.VMEM((N * ROWS, F), BF16),
             pltpu.VMEM((F, D), BF16),
             pltpu.VMEM((D, F), BF16),
             pltpu.VMEM((D, F), BF16),
             pltpu.VMEM((N, 16, ROWS, D), BF16),
-            pltpu.VMEM((N, 16, ROWS, D), BF16),
             pltpu.VMEM((N, D, 16 * ROWS), BF16),
-            pltpu.VMEM((12, N, N, ROWS, F), BF16),
             pltpu.VMEM((N, N, N, ROWS, F), F32),
             pltpu.VMEM((3, N, 2, N, ROWS, HALF), BF16),
             pltpu.VMEM((3, N, 2, N, ROWS, HALF), BF16),
@@ -444,7 +448,7 @@
             pltpu.VMEM((N, N, 2, 2, ROWS, D), F32),
             pltpu.VMEM((N, N, 2, ROWS, D), F32),
             pltpu.VMEM((N, 3, 2, ROWS, D), F32),
-            dma((3,)),
+            dma((7,)),
             dma((N, 7)),
             dma((N, 7)),
             dma((7,)),
@@ -457,7 +461,7 @@
             dma((4, N)),
         ],
         compiler_params=pltpu.CompilerParams(
-            collective_id=0, has_side_effects=True, vmem_limit_bytes=51 << 20
+            collective_id=0, has_side_effects=True, vmem_limit_bytes=38 << 20
         ),
         cost_estimate=pl.CostEstimate(
             flops=6 * 1024 * D * F, bytes_accessed=20 << 20, transcendentals=64 * F
@@ -466,32 +470,59 @@
     )(out_grad, inputs, gate_pre, up_pre, gate_weight, up_weight, down_weight)
 
 
-def _write(a, b, c, d, a_out, b_out, c_out, d_out, sem):
-    copies = []
-    for i, (src, dst) in enumerate(((b, b_out), (c, c_out), (d, d_out), (a, a_out))):
-        copies.append(pltpu.make_async_copy(src, dst, sem.at[i]))
-        copies[i].start()
+def _finish(ig, gg, ug, arr, og, ig_out, gg_out, ug_out, dg_out, total, sem, tile_sem):
+    copies = [
+        pltpu.make_async_copy(gg, gg_out, sem.at[0]),
+        pltpu.make_async_copy(ug, ug_out, sem.at[1]),
+        pltpu.make_async_copy(ig, ig_out, sem.at[2]),
+    ]
+    for copy in copies:
+        copy.start()
+
+    def tile_copy(n):
+        at_n = pl.ds(pl.multiple_of(n * TILE, TILE), TILE)
+        return pltpu.make_async_copy(total.at[at_n], dg_out.at[at_n], tile_sem.at[n])
+
+    @pl.loop(0, F // TILE)
+    def _(n):
+        at_n = pl.ds(pl.multiple_of(n * TILE, TILE), TILE)
+        out = None
+        for slot, j in ((0, 0), (1, 1), (10, 2), (11, 3)):
+            lhs = arr[slot, :, :, :, at_n].reshape(16 * ROWS, TILE)
+            rhs = og[j].reshape(16 * ROWS, D)
+            product = lax.dot_general(lhs, rhs, TN, preferred_element_type=F32)
+            out = product if out is None else out + product
+        total[at_n, :] = out
+        tile_copy(n).start()
+
+    @pl.loop(0, F // TILE)
+    def _(n):
+        tile_copy(n).wait()
+
     for copy in copies:
         copy.wait()
 
 
-def write(*grads):
-    grads = [pltpu.with_memory_space_constraint(g, pltpu.VMEM) for g in grads]
-    hbm = pl.BlockSpec(memory_space=pl.ANY)
+def finish(*values):
+    values = [pltpu.with_memory_space_constraint(v, pltpu.VMEM) for v in values]
     return pl.pallas_call(
-        _write,
-        out_shape=[pltpu.HBM(g.shape, g.dtype) for g in grads],
-        in_specs=[pl.BlockSpec(memory_space=pltpu.VMEM)] * 4,
-        out_specs=[hbm] * 4,
-        scratch_shapes=[pltpu.SemaphoreType.DMA((4,))],
-        compiler_params=pltpu.CompilerParams(vmem_limit_bytes=2 << 20),
-        name="write",
-    )(*grads)
+        _finish,
+        out_shape=[pltpu.HBM(v.shape, v.dtype) for v in values[:3]] + [pltpu.HBM((F, D), F32)],
+        in_specs=[pl.BlockSpec(memory_space=pltpu.VMEM)] * 5,
+        out_specs=[pl.BlockSpec(memory_space=pl.ANY)] * 4,
+        scratch_shapes=[
+            pltpu.VMEM((F, D), F32),
+            pltpu.SemaphoreType.DMA((3,)),
+            pltpu.SemaphoreType.DMA((F // TILE,)),
+        ],
+        compiler_params=pltpu.CompilerParams(vmem_limit_bytes=12 << 20),
+        name="finish",
+    )(*values)
 
 
 def body(inputs, out_grad, gate_pre, up_pre, gate_weight, up_weight, down_weight):
-    grads = exchange(out_grad, inputs, gate_pre, up_pre, gate_weight, up_weight, down_weight)
-    return tuple(write(*grads))
+    values = exchange(out_grad, inputs, gate_pre, up_pre, gate_weight, up_weight, down_weight)
+    return tuple(finish(*values))
 
 
 def solution(mesh):

time: 113 us -> 106 us (0.938)
  Pallas kernels: 111 us -> 105 us
    pallas_call x1, Pallas kernels: 107 us -> 101 us  [exchange(): pl.pallas_call(_exchange, out_shape=(pltpu.VMEM((128, D), F32), pltpu.VME...]
where the time goes in v4:
time: 106 us
  Pallas kernels  105 us (99%)
    pallas_call x1, Pallas kernels, exchange(): pl.pallas_call(_exchange, out_shape=(pltpu.VMEM((128, D), F32), pltpu.VME...  101 us
    pallas_call x1, Pallas kernels, finish(): pl.pallas_call(_finish, out_shape=[pltpu.HBM(v.shape, v.dtype) for v in v...  4.33 us

profile of v4, /device:TPU:0, one launch (start us, length us, event | category | flops | bytes accessed | tf_op | source)
XLA Modules:
  0.0 105.5 jit_solution(12582412707276802521)
XLA Ops:
  0.6 100.6 %exchange.1 = (f32[128,512]{1,0:T(8,128)S(1)}, f32[512,1792]{1,0:T(8,128)S(1)}, f32[512,1792]{1,0:T(8,128)S(1)}, bf16[12,4,4,16,1792]{4,3,2,1,0:T(8,128)(2,1)S(1)}, bf16[4,16,16,512]{3,2,1,0:T(8,128)(2,1)S(1)}) custom-call(bf16[128,512]{1,0:T(8,128)(2,1)} %og_hbm.1, bf16[128,512]{1,0:T(8,128)(2,1)} %in_hbm.1, bf16[64,1792]{1,0:T(8,128)(2,1)} %gate_hbm.1, ...), custom_call_target="tpu_custom_call" | custom-call | flops 5637144576 | bytes 20971520 | tf_op jit(solution)/shard_map/exchange/pallas_call | solution.py:422
  101.2 4.3 %finish.1 = (f32[128,512]{1,0:T(8,128)}, f32[512,1792]{1,0:T(8,128)}, f32[512,1792]{1,0:T(8,128)}, f32[1792,512]{1,0:T(8,128)}) custom-call(f32[128,512]{1,0:T(8,128)S(1)} %get-tuple-element.9.ig, f32[512,1792]{1,0:T(8,128)S(1)} %get-tuple-element.10.gg, f32[512,1792]{1,0:T(8,128)S(1)} %get-tuple-element.11.ug, ...), custom_call_target="tpu_custom_call" | custom-call | tf_op jit(solution)/shard_map/finish/pallas_call | solution.py:508

commit v5 on v4

--- a/solution.py
+++ b/solution.py
@@ -299,14 +299,12 @@
 
     def wg(j):
         first = slots(j)
-        for ref, slot in ((gg_ref, first), (ug_ref, first + 1)):
-
-            @pl.loop(0, F // TILE)
-            def _(n):
-                at_n = pl.ds(pl.multiple_of(n * TILE, TILE), TILE)
+        @pl.loop(0, F // TILE)
+        def _(n):
+            at_n = pl.ds(pl.multiple_of(n * TILE, TILE), TILE)
+            for ref, slot in ((gg_ref, first), (ug_ref, first + 1)):
                 rhs = arr[slot, :, :, :, at_n].reshape(16 * ROWS, TILE)
                 out = jnp.dot(in_t[j], rhs, preferred_element_type=F32)
-
                 ref[:, at_n] = jnp.where(j > 0, ref[:, at_n], 0.0) + out
 
     def turn(j):
@@ -336,13 +334,6 @@
         def _():
             call(j)
 
-    def ag_stage(t, number, call):
-        v = t - number
-
-        @pl.when(((v >= 0) & (v < N)) | (v == N + 1))
-        def _():
-            call(v)
-
     def ag_sent(v):
         for s in range(2):
             for kind in range(8):
@@ -355,57 +346,68 @@
                     rs(kind, j, s, o, True).wait_send()
         ag_sent(j)
 
+    def once(t, number, *calls):
+        @pl.when(t == number)
+        def _():
+            for call, v in calls:
+                call(v)
+
+    def weights_here(_):
+        loads[5].wait()
+        loads[6].wait()
+
+    def inputs_here(_):
+        for step in range(1, 8):
+            in_copy(step, (col + 8 - step) % 8).wait_recv()
+
+    def gathered_sent(_):
+        for j in range(N):
+            for step in range(1, 8):
+                og_copy(j, step, col).wait_send()
+        for step in range(1, 8):
+            in_copy(step, col).wait_send()
+        ag_sent(-6)
+
     @pl.loop(0, 14)
     def _(t):
+        once(t, 9, (weights_here, 0))
+        stage(t, 9, N, ig_i0)
+        stage(t, 6, N, ag_a2)
+        once(t, 6, (inputs_here, 0))
+        stage(t, 6, N, turn)
+        once(t, 7, (ag_a4, -6))
+
+        @pl.when((t == 10) | (t == 13))
+        def _():
+            wg((t - 10) // 3)
+
+        stage(t, 5, N, ag_a1)
+        stage(t, 0, N, rs_s0)
+        once(t, 0, (ag_a1, 4))
+        stage(t, 1, N, rs_s1)
+        stage(t, 10, N, ig_i1)
+        stage(t, 2, N, rs_s2)
+        stage(t, 3, N, rs_s3)
+        once(t, 6, (ag_a3, -6))
+        stage(t, 7, N, ag_a3)
         stage(t, 4, N, rs_s4)
-        stage(t, 3, N, rs_s3)
-        stage(t, 2, N, rs_s2)
-        stage(t, 1, N, rs_s1)
-        stage(t, 0, N, rs_s0)
-
-        @pl.when(t == 0)
-        def _():
-            ag_a2(-6)
-
-        @pl.when(t == 1)
-        def _():
-            ag_a3(-6)
-
-        @pl.when(t == 7)
-        def _():
-            loads[5].wait()
-            loads[6].wait()
-
-        ag_stage(t, 5, ag_a1)
-        ag_stage(t, 6, ag_a2)
-        ag_stage(t, 7, ag_a3)
-        @pl.when(t == 7)
-        def _():
-            for step in range(1, 8):
-                in_copy(step, (col + 8 - step) % 8).wait_recv()
-
-        stage(t, 7, N, turn)
-
-        stage(t, 9, N, ig_i1)
-        @pl.when(t == 8)
-        def _():
-            ag_a4(-6)
-
-        stage(t, 9, N, wg)
-
-        @pl.when(t == 9)
-        def _():
-            for j in range(N):
-                for step in range(1, 8):
-                    og_copy(j, step, col).wait_send()
-            for step in range(1, 8):
-                in_copy(step, col).wait_send()
-            ag_sent(-6)
-
-        stage(t, 10, N, sent)
+        once(t, 10, (ag_a2, 4))
+        once(t, 4, (ag_a2, -6))
         stage(t, 8, N, ag_a4)
-        stage(t, 8, N, ig_i0)
-        stage(t, 10, N, ig_i2)
+        once(t, 9, (gathered_sent, 0))
+        stage(t, 10, N - 1, sent)
+
+    ag_a3(4)
+
+    @pl.loop(2, N)
+    def _(j):
+        wg(j)
+
+    sent(3)
+
+    @pl.loop(0, N)
+    def _(j):
+        ig_i2(j)
 
     ag_a4(4)
     for j in range(N):

time: 106 us -> 103 us (0.972)
  Pallas kernels: 105 us -> 102 us
    pallas_call x1, Pallas kernels: 101 us -> 97.9 us  [exchange(): pl.pallas_call(_exchange, out_shape=(pltpu.VMEM((128, D), F32), pltpu.VME...]
where the time goes in v5:
time: 103 us
  Pallas kernels  102 us (99%)
    pallas_call x1, Pallas kernels, exchange(): pl.pallas_call(_exchange, out_shape=(pltpu.VMEM((128, D), F32), pltpu.VME...  97.9 us
    pallas_call x1, Pallas kernels, finish(): pl.pallas_call(_finish, out_shape=[pltpu.HBM(v.shape, v.dtype) for v in v...  4.33 us

profile of v5, /device:TPU:0, one launch (start us, length us, event | category | flops | bytes accessed | tf_op | source)
XLA Modules:
  0.0 102.9 jit_solution(2083044528332275876)
XLA Ops:
  0.6 97.9 %exchange.1 = (f32[128,512]{1,0:T(8,128)S(1)}, f32[512,1792]{1,0:T(8,128)S(1)}, f32[512,1792]{1,0:T(8,128)S(1)}, bf16[12,4,4,16,1792]{4,3,2,1,0:T(8,128)(2,1)S(1)}, bf16[4,16,16,512]{3,2,1,0:T(8,128)(2,1)S(1)}) custom-call(bf16[128,512]{1,0:T(8,128)(2,1)} %og_hbm.1, bf16[128,512]{1,0:T(8,128)(2,1)} %in_hbm.1, bf16[64,1792]{1,0:T(8,128)(2,1)} %gate_hbm.1, ...), custom_call_target="tpu_custom_call" | custom-call | flops 5637144576 | bytes 20971520 | tf_op jit(solution)/shard_map/exchange/pallas_call | solution.py:424
  98.5 4.3 %finish.1 = (f32[128,512]{1,0:T(8,128)}, f32[512,1792]{1,0:T(8,128)}, f32[512,1792]{1,0:T(8,128)}, f32[1792,512]{1,0:T(8,128)}) custom-call(f32[128,512]{1,0:T(8,128)S(1)} %get-tuple-element.9.ig, f32[512,1792]{1,0:T(8,128)S(1)} %get-tuple-element.10.gg, f32[512,1792]{1,0:T(8,128)S(1)} %get-tuple-element.11.ug, ...), custom_call_target="tpu_custom_call" | custom-call | tf_op jit(solution)/shard_map/finish/pallas_call | solution.py:510

commit v6 on v5

--- a/solution.py
+++ b/solution.py
@@ -474,10 +474,11 @@
 
 def _finish(ig, gg, ug, arr, og, ig_out, gg_out, ug_out, dg_out, total, sem, tile_sem):
     copies = [
-        pltpu.make_async_copy(gg, gg_out, sem.at[0]),
-        pltpu.make_async_copy(ug, ug_out, sem.at[1]),
-        pltpu.make_async_copy(ig, ig_out, sem.at[2]),
+        pltpu.make_async_copy(src.at[part], dst.at[part], sem.at[i, p])
+        for p, part in enumerate(pl.ds(128 * p, 128) for p in range(N))
+        for i, (src, dst) in enumerate(((gg, gg_out), (ug, ug_out)))
     ]
+    copies.append(pltpu.make_async_copy(ig, ig_out, sem.at[2, 0]))
     for copy in copies:
         copy.start()
 
@@ -514,7 +515,7 @@
         out_specs=[pl.BlockSpec(memory_space=pl.ANY)] * 4,
         scratch_shapes=[
             pltpu.VMEM((F, D), F32),
-            pltpu.SemaphoreType.DMA((3,)),
+            pltpu.SemaphoreType.DMA((3, N)),
             pltpu.SemaphoreType.DMA((F // TILE,)),
         ],
         compiler_params=pltpu.CompilerParams(vmem_limit_bytes=12 << 20),

time: 103 us -> 103 us (level)
  no operation moved by 1% of the time
where the time goes in v6:
time: 103 us
  Pallas kernels  102 us (99%)
    pallas_call x1, Pallas kernels, exchange(): pl.pallas_call(_exchange, out_shape=(pltpu.VMEM((128, D), F32), pltpu.VME...  97.9 us
    pallas_call x1, Pallas kernels, finish(): pl.pallas_call(_finish, out_shape=[pltpu.HBM(v.shape, v.dtype) for v in v...  4.34 us

profile of v6, /device:TPU:0, one launch (start us, length us, event | category | flops | bytes accessed | tf_op | source)
XLA Modules:
  0.0 102.9 jit_solution(6962739707643575184)
XLA Ops:
  0.6 97.9 %exchange.1 = (f32[128,512]{1,0:T(8,128)S(1)}, f32[512,1792]{1,0:T(8,128)S(1)}, f32[512,1792]{1,0:T(8,128)S(1)}, bf16[12,4,4,16,1792]{4,3,2,1,0:T(8,128)(2,1)S(1)}, bf16[4,16,16,512]{3,2,1,0:T(8,128)(2,1)S(1)}) custom-call(bf16[128,512]{1,0:T(8,128)(2,1)} %og_hbm.1, bf16[128,512]{1,0:T(8,128)(2,1)} %in_hbm.1, bf16[64,1792]{1,0:T(8,128)(2,1)} %gate_hbm.1, ...), custom_call_target="tpu_custom_call" | custom-call | flops 5637144576 | bytes 20971520 | tf_op jit(solution)/shard_map/exchange/pallas_call | solution.py:424
  98.5 4.3 %finish.1 = (f32[128,512]{1,0:T(8,128)}, f32[512,1792]{1,0:T(8,128)}, f32[512,1792]{1,0:T(8,128)}, f32[1792,512]{1,0:T(8,128)}) custom-call(f32[128,512]{1,0:T(8,128)S(1)} %get-tuple-element.9.ig, f32[512,1792]{1,0:T(8,128)S(1)} %get-tuple-element.10.gg, f32[512,1792]{1,0:T(8,128)S(1)} %get-tuple-element.11.ug, ...), custom_call_target="tpu_custom_call" | custom-call | tf_op jit(solution)/shard_map/finish/pallas_call | solution.py:511
